TPU v7x, 128 devices: a whole 4x4x4 slice. The times are simulated.
128 devices in a mesh: row: 8 (over z, core), col: 16 (over y, x).
Axes of the slice: x: 4, y: 4, z: 4, core: 2. Of those that a mesh axis runs over, the one named last changes fastest.
Arguments:
- rest_pos: float32 [3, 262144], P(None, ('row', 'col')), may hold values from 0 to 4
- displacement: float32 [3, 262144], P(None, ('row', 'col')), may hold values from -1.2 to 1.2
- velocity: float32 [3, 262144], P(None, ('row', 'col')), may hold values from -3 to 3
- accel_prev: float32 [3, 262144], P(None, ('row', 'col')), may hold values from -6 to 6
- material: int32 [262144], P(('row', 'col')), may hold values from 0 to 1
- moduli: float32 [2], replicated, may hold values from 0.25 to 4
- pair_owner: int32 [16384], P(('row', 'col')), may hold values from 0 to 255, as said below
- pair_partner: int32 [16384], P(('row', 'col')), may hold values from 0 to 127, as said below
- pair_count: int32 [128], P(('row', 'col')), may hold values from 16 to 128, as said below
- bond_mask: int32 [16384, 128, 128], P(('row', 'col')), may hold values 0 or 1
- broken: int32 [16384, 128, 128], P(('row', 'col')), may hold values 0 or 1
Outputs:
- disp_out: float32 [3, 262144], P(None, ('row', 'col'))
- vel_out: float32 [3, 262144], P(None, ('row', 'col'))
Inputs may be any that keep to these rules, and one draw needn't show every extreme that they name: `pair_owner`: on each device the 128 slots name distinct tile pairs; over all devices no two tiles are joined by more than one slot, and no tile is joined with itself. `pair_partner`: drawn together with pair_owner. A device's live slots are its first pair_count slots; the lists and masks of the other slots are to be ignored. Some device has all 128 slots live.
All inputs are finite; a program needn't handle non-finite values. No bound on the sum of `bond_mask` or of `broken` on one device may be relied on, other than what follows from the above.
Results may differ from a plain program's by a relative error of at most 0.00011.
Values sent between devices are 32-bit elements; how exact they have to be, the bound alone decides.
No kernel may reach another device: no remote copies, remote signals or barrier semaphores. Data moves between devices by JAX's collectives and lax.ppermute only.
A program may use at most 64 MiB of HBM per device.

v0:
```python
import math

import jax
import jax.numpy as jnp
from jax import lax
from jax.sharding import PartitionSpec as P

TILE = 128
TILE_DEV = 16
STEPS = 2
PAIRS_DEV = 128


RADIUS = 1.0
TIME_STEP = 0.5
FIBER_GAIN = 8.0
BLOCK_PAIRS = 8


def bond_terms(owners, others, weight, strength):
    rest_vec = [
        others[component][:, None, :] - owners[component][:, :, None] for component in range(3)
    ]
    current = [
        rest_vec[component] + others[component + 3][:, None, :] - owners[component + 3][:, :, None]
        for component in range(3)
    ]
    rest_len = jnp.sqrt(
        rest_vec[0] * rest_vec[0]
        + rest_vec[1] * rest_vec[1]
        + rest_vec[2] * rest_vec[2]
        + RADIUS * RADIUS
    )
    cur_len = jnp.sqrt(
        current[0] * current[0]
        + current[1] * current[1]
        + current[2] * current[2]
        + RADIUS * RADIUS
    )
    stretch = (cur_len - rest_len) / rest_len
    axial_cos = rest_vec[0] / rest_len
    stiffness = jnp.sqrt(owners[6][:, :, None] * others[6][:, None, :]) * (
        1.0 + FIBER_GAIN * owners[7][:, :, None] * others[7][:, None, :] * axial_cos * axial_cos
    )
    factor = strength * weight * stiffness * stretch / cur_len
    on_owner = jnp.stack([jnp.sum(factor * current[component], axis=2) for component in range(3)])
    on_partner = jnp.stack(
        [-jnp.sum(factor * current[component], axis=1) for component in range(3)]
    )
    return (on_owner, on_partner)


def ghost_blocks(state_rows):
    row_block = lax.all_gather(state_rows, "col", axis=1, tiled=True)
    col_block = lax.all_gather(state_rows, "row", axis=1, tiled=True)
    return (row_block, col_block)


def tile_forces(state_rows, strength):
    tile_count = state_rows.shape[1]
    group_size = math.gcd(tile_count, BLOCK_PAIRS)

    def add_group(block_id, summed):
        first_slot = block_id * group_size
        tile_set = lax.dynamic_slice_in_dim(state_rows, first_slot, group_size, 1)
        weight = jnp.ones((group_size, TILE, TILE), jnp.float32)
        on_owner, unused_part = bond_terms(tile_set, tile_set, weight, strength)
        updated = lax.dynamic_slice_in_dim(summed, first_slot, group_size, 1) + on_owner
        return lax.dynamic_update_slice_in_dim(summed, updated, first_slot, 1)

    return lax.fori_loop(
        0, tile_count // group_size, add_group, jnp.zeros((3, tile_count, TILE), jnp.float32)
    )


def pair_forces(
    row_block, col_block, pair_owner, pair_partner, live_count, bond_mask, broken, strength
):
    row_force = jnp.zeros((3, row_block.shape[1], TILE), jnp.float32)
    col_force = jnp.zeros((3, col_block.shape[1], TILE), jnp.float32)

    def add_block(block_id, forces):
        first_slot = block_id * BLOCK_PAIRS
        owner_ids = lax.dynamic_slice_in_dim(pair_owner, first_slot, BLOCK_PAIRS)
        partner_ids = lax.dynamic_slice_in_dim(pair_partner, first_slot, BLOCK_PAIRS)
        bonds = lax.dynamic_slice_in_dim(bond_mask, first_slot, BLOCK_PAIRS)
        cracks = lax.dynamic_slice_in_dim(broken, first_slot, BLOCK_PAIRS)
        live_part = (first_slot + jnp.arange(BLOCK_PAIRS, dtype=jnp.int32) < live_count).astype(
            jnp.int32
        )
        weight = (bonds * (1 - cracks) * live_part[:, None, None]).astype(jnp.float32)
        owners = jnp.take(row_block, owner_ids, axis=1)
        others = jnp.take(col_block, partner_ids, axis=1)
        on_owner, on_partner = bond_terms(owners, others, weight, strength)
        return (
            forces[0].at[:, owner_ids].add(on_owner),
            forces[1].at[:, partner_ids].add(on_partner),
        )

    blocks = pair_owner.shape[0] // BLOCK_PAIRS
    return lax.fori_loop(0, blocks, add_block, (row_force, col_force))


def reduce_forces(row_force, col_force, tile_count):
    row_whole = lax.psum(row_force, "col")
    col_whole = lax.psum(col_force, "row")
    from_rows = lax.dynamic_slice_in_dim(
        row_whole, lax.axis_index("col") * tile_count, tile_count, 1
    )
    from_cols = lax.dynamic_slice_in_dim(
        col_whole, lax.axis_index("row") * tile_count, tile_count, 1
    )
    return from_rows + from_cols


def per_device(
    rest_pos,
    displacement,
    velocity,
    accel_prev,
    material,
    moduli,
    pair_owner,
    pair_partner,
    pair_count,
    bond_mask,
    broken,
):
    strength = 1.5 / math.sqrt(TILE * (1.0 + PAIRS_DEV / TILE_DEV))
    tile_count = material.shape[0] // TILE
    fibrous = material.astype(jnp.float32)
    modulus = jnp.where(material == 1, moduli[1], moduli[0])
    live_count = pair_count[0]
    displaced = displacement
    moving = velocity
    acceleration = accel_prev
    for step_id in range(STEPS):
        moving = moving + 0.5 * TIME_STEP * acceleration
        displaced = displaced + TIME_STEP * moving
        state_rows = jnp.concatenate(
            [rest_pos, displaced, modulus[None], fibrous[None]], 0
        ).reshape(8, tile_count, TILE)
        row_block, col_block = ghost_blocks(state_rows)
        own_force = tile_forces(state_rows, strength)
        row_force, col_force = pair_forces(
            row_block, col_block, pair_owner, pair_partner, live_count, bond_mask, broken, strength
        )
        summed = own_force + reduce_forces(row_force, col_force, tile_count)
        acceleration = summed.reshape(3, tile_count * TILE)
        moving = moving + 0.5 * TIME_STEP * acceleration
    return (displaced, moving)


def solution(mesh):
    placed = (
        P(None, ("row", "col")),
        P(None, ("row", "col")),
        P(None, ("row", "col")),
        P(None, ("row", "col")),
        P(("row", "col")),
        P(),
        P(("row", "col")),
        P(("row", "col")),
        P(("row", "col")),
        P(("row", "col"), None, None),
        P(("row", "col"), None, None),
    )
    return jax.shard_map(
        per_device,
        mesh=mesh,
        in_specs=placed,
        out_specs=(P(None, ("row", "col")), P(None, ("row", "col"))),
        check_vma=False,
    )
```

profile of v0, /device:TPU:0, one launch (start us, length us, event | category | flops | bytes accessed | tf_op | source)
XLA Modules:
  0.0 692.8 jit_solution(15594150649838245112)
XLA Ops:
  13.5 14.6 %all_gather.13 = f32[8,128,128]{2,0,1:T(8,128)S(1)} all-gather(f32[8,16,128]{2,0,1:T(8,128)} %pad_maximum_fusion.1), channel_id=1, replica_groups=mesh['row'=8,'col'=16] {'row'}, dimensions={1}, use_global_device_ids=true | all-gather | bytes 589824 | tf_op jit(solution)/shard_map/all_gather | solution.py:55
  28.1 30.5 %all-gather.3.cloned.1.call-done = f32[8,256,128]{2,0,1:T(8,128)} async-done(((f32[8,16,128]{2,0,1:T(8,128)}), f32[8,256,128]{2,0,1:T(8,128)}) %all-gather.3.cloned.1.call-update) | async-done | bytes 1048592 | tf_op jit(solution)/shard_map/all_gather | solution.py:54
  58.8 149.6 %while.57 = (s32[]{:T(128)}, f32[3,256,128]{2,0,1:T(4,128)S(1)}, f32[3,128,128]{2,0,1:T(4,128)S(1)}, s32[128]{0:T(128)}, s32[128,128,128]{2,1,0:T(8,128)}, /*ind...) while((s32[]{:T(128)}, f32[3,256,128]{2,0,1:T(4,128)S(1)}, ...), condition=%wide.region_14.17_spmd, body=%wide.region_5.16_spmd.sunk | while | flops 6195326 | bytes 1688171 | solution.py:101
  62.8 3.7 fusion.128
  72.2 3.7 fusion.128
  81.5 3.7 fusion.128
  90.9 3.7 fusion.128
  100.2 3.7 fusion.128
  109.6 3.7 fusion.128
  118.9 3.7 fusion.128
  128.3 3.7 fusion.128
  137.6 3.7 fusion.128
  147.0 3.7 fusion.128
  156.3 3.7 fusion.128
  165.7 3.7 fusion.128
  175.0 3.7 fusion.128
  184.4 3.7 fusion.128
  193.7 3.7 fusion.128
  203.1 3.7 fusion.128
  210.1 4.5 while.56
  210.1 2.1 fusion.124
  212.4 2.1 fusion.124
  214.5 54.0 %all-reduce.7.cloned.1.call-done = f32[3,128,128]{2,1,0:T(8,128)} async-done(((f32[3,128,128]{2,1,0:T(8,128)}), f32[3,128,128]{2,1,0:T(8,128)}) %all-reduce.7.cloned.1.call-update) | async-done | bytes 196624 | tf_op jit(solution)/shard_map/psum | solution.py:106
  268.5 86.6 %all-reduce.5.cloned.1.call-done = f32[3,256,128]{2,1,0:T(8,128)} async-done(((f32[3,256,128]{2,1,0:T(8,128)}), f32[3,256,128]{2,1,0:T(8,128)}) %all-reduce.5.cloned.1.call-update) | async-done | bytes 393232 | tf_op jit(solution)/shard_map/psum | solution.py:105
  356.7 13.8 %all_gather.15 = f32[8,128,128]{2,0,1:T(8,128)S(1)} all-gather(f32[8,16,128]{2,0,1:T(8,128)} %pad_maximum_fusion), channel_id=1, replica_groups=mesh['row'=8,'col'=16] {'row'}, dimensions={1}, use_global_device_ids=true | all-gather | bytes 589824 | tf_op jit(solution)/shard_map/all_gather | solution.py:55
  370.5 28.9 %all-gather.5.cloned.1.call-done = f32[8,256,128]{2,0,1:T(8,128)} async-done(((f32[8,16,128]{2,0,1:T(8,128)}), f32[8,256,128]{2,0,1:T(8,128)}) %all-gather.5.cloned.1.call-update) | async-done | bytes 1048592 | tf_op jit(solution)/shard_map/all_gather | solution.py:54
  399.5 138.8 %while.59 = (s32[]{:T(128)}, f32[3,256,128]{2,0,1:T(4,128)S(1)}, f32[3,128,128]{2,0,1:T(4,128)S(1)}, s32[128]{0:T(128)S(1)}, s32[128,128,128]{2,1,0:T(8,128)}, /...) while((s32[]{:T(128)}, f32[3,256,128]{2,0,1:T(4,128)S(1)}, ...), condition=%wide.region_31.34_spmd, body=%wide.region_22.33_spmd.sunk | while | flops 6195326 | bytes 1688171 | solution.py:101
  402.8 3.7 fusion.133
  411.5 3.7 fusion.133
  420.2 3.7 fusion.133
  428.9 3.7 fusion.133
  437.5 3.7 fusion.133
  446.2 3.7 fusion.133
  454.9 3.7 fusion.133
  463.6 3.7 fusion.133
  472.2 3.7 fusion.133
  480.9 3.7 fusion.133
  489.6 3.7 fusion.133
  498.3 3.7 fusion.133
  506.9 3.7 fusion.133
  515.6 3.7 fusion.133
  524.3 3.7 fusion.133
  533.0 3.7 fusion.133
  539.9 4.5 while.58
  540.0 2.1 fusion.129
  542.2 2.1 fusion.129
  544.4 54.0 %all-reduce.11.cloned.1.call-done = f32[3,128,128]{2,1,0:T(8,128)} async-done(((f32[3,128,128]{2,1,0:T(8,128)}), f32[3,128,128]{2,1,0:T(8,128)}) %all-reduce.11.cloned.1.call-update) | async-done | bytes 196624 | tf_op jit(solution)/shard_map/psum | solution.py:106
  598.4 86.1 %all-reduce.9.cloned.1.call-done = f32[3,256,128]{2,1,0:T(8,128)} async-done(((f32[3,256,128]{2,1,0:T(8,128)}), f32[3,256,128]{2,1,0:T(8,128)}) %all-reduce.9.cloned.1.call-update) | async-done | bytes 393232 | tf_op jit(solution)/shard_map/psum | solution.py:105
  (606 shorter events, 179.7 us)
Async XLA Ops:
  7.2 51.5 %all-gather.3.cloned.1.call-start = ((), (), s32[]{:S(2)}) async-start(), calls=%async_computation | async-start | bytes 1114112 | tf_op jit(solution)/shard_map/all_gather | solution.py:54
  13.4 196.6 %copy-start.1 = (f32[8,16,128]{2,0,1:T(8,128)S(1)}, f32[8,16,128]{2,0,1:T(8,128)}, u32[]{:S(2)}) copy-start(f32[8,16,128]{2,0,1:T(8,128)} %pad_maximum_fusion.1) | copy-start | bytes 196612
  13.5 255.0 %all-reduce.7.cloned.1.call-start = ((), (), s32[]{:S(2)}) async-start(), calls=%async_computation.2 | async-start | bytes 393216 | tf_op jit(solution)/shard_map/psum | solution.py:106
  58.7 297.1 %copy-start.2 = (f32[3,2048]{1,0:T(4,128)S(1)}, f32[3,2048]{1,0:T(4,128)}, u32[]{:S(2)}) copy-start(f32[3,2048]{1,0:T(4,128)} %param.25) | copy-start | bytes 73732
  58.7 297.1 %copy-start.3 = (f32[3,2048]{1,0:T(4,128)S(1)}, f32[3,2048]{1,0:T(4,128)}, u32[]{:S(2)}) copy-start(f32[3,2048]{1,0:T(4,128)} %param.26) | copy-start | bytes 73732
  58.8 297.1 %copy-start.4 = (f32[3,2048]{1,0:T(4,128)S(1)}, f32[3,2048]{1,0:T(4,128)}, u32[]{:S(2)}) copy-start(f32[3,2048]{1,0:T(4,128)} %param.24) | copy-start | bytes 73732
  58.8 297.2 %copy-start.6 = (f32[3,2048]{1,0:T(4,128)S(1)}, f32[3,2048]{1,0:T(4,128)}, u32[]{:S(2)}) copy-start(f32[3,2048]{1,0:T(4,128)} %param.23) | copy-start | bytes 73732
  208.4 191.1 %copy-start.7 = (s32[128]{0:T(128)S(1)}, s32[128]{0:T(128)}, u32[]{:S(2)}) copy-start(s32[128]{0:T(128)} %get-tuple-element.1138) | copy-start | bytes 1540
  208.4 191.1 %copy-start.8 = (s32[128]{0:T(128)S(1)}, s32[128]{0:T(128)}, u32[]{:S(2)}) copy-start(s32[128]{0:T(128)} %get-tuple-element.1139) | copy-start | bytes 1540
  209.1 146.0 %all-reduce.5.cloned.1.call-start = ((), (), s32[]{:S(2)}) async-start(), calls=%async_computation.1 | async-start | bytes 786432 | tf_op jit(solution)/shard_map/psum | solution.py:105
  210.0 189.4 %all-gather.5.cloned.1.call-start = ((), (), s32[]{:S(2)}) async-start(), calls=%async_computation.3 | async-start | bytes 1114112 | tf_op jit(solution)/shard_map/all_gather | solution.py:54
  355.9 184.0 %copy-start.5 = (f32[3,2048]{1,0:T(4,128)}, f32[3,2048]{1,0:T(4,128)S(1)}, u32[]{:S(2)}) copy-start(f32[3,2048]{1,0:T(4,128)S(1)} %multiply_add_fusion) | copy-start | bytes 73732
  356.6 183.3 %copy-start = (f32[8,16,128]{2,0,1:T(8,128)S(1)}, f32[8,16,128]{2,0,1:T(8,128)}, u32[]{:S(2)}) copy-start(f32[8,16,128]{2,0,1:T(8,128)} %pad_maximum_fusion) | copy-start | bytes 196612
  356.6 241.8 %all-reduce.11.cloned.1.call-start = ((), (), s32[]{:S(2)}) async-start(), calls=%async_computation.5 | async-start | bytes 393216 | tf_op jit(solution)/shard_map/psum | solution.py:106
  539.0 145.5 %all-reduce.9.cloned.1.call-start = ((), (), s32[]{:S(2)}) async-start(), calls=%async_computation.4 | async-start | bytes 786432 | tf_op jit(solution)/shard_map/psum | solution.py:105
Sparse Core Ops, SparseCore 0:
  13.6 45.0 all-gather.2
  209.3 59.1 all-reduce.6
  272.1 82.9 all-reduce.4
  357.3 41.9 all-gather.4
  539.1 59.2 all-reduce.10
  601.5 82.9 all-reduce.8
where the time goes:
time: 697 us; the launch traced here: 693 us
  waiting for transfers between devices  340 us (49%)
  other arithmetic  225 us (32%)
  local copies, waits for them, and re-layouts  80 us (11%)
  blocking collectives  28.4 us (4%)
  between operations  14.3 us (2%)
    psum x2, waiting for transfers between devices, reduce_forces(): row_whole = lax.psum(row_force, 'col')  173 us
    reduce_sum x32, other arithmetic, bond_terms(): jnp.sum(factor * current[component], axis=1)  117 us
    psum x2, waiting for transfers between devices, reduce_forces(): col_whole = lax.psum(col_force, 'row')  108 us
    all_gather x2, waiting for transfers between devices, ghost_blocks(): row_block = lax.all_gather(state_rows, 'col', axis=1, tiled=True)  59.4 us
    gather x32, local copies, waits for them, and re-layouts, add_block(): owners = jnp.take(row_block, owner_ids, axis=1)  56.8 us
    all_gather x2, blocking collectives, ghost_blocks(): col_block = lax.all_gather(state_rows, 'row', axis=1, tiled=True)  28.4 us
    scatter-add x32, other arithmetic, add_block(): forces[1].at[:, partner_ids].add(on_partner)  24.9 us
    scatter-add x32, other arithmetic, add_block(): forces[0].at[:, owner_ids].add(on_owner)  24.9 us
  transfers between devices with their start and end apart: 6, of which 6 were waited for; matrix products, arithmetic and copies ran while one was open for 1% of the time, Pallas kernels for 0%

commit v1 on v0

v1 whole, which is shorter than its diff:
```python
import math, functools
import jax, jax.numpy as jnp
from jax import lax
from jax.sharding import PartitionSpec as P
from jax.experimental import pallas as pl
from jax.experimental.pallas import tpu as pltpu

TILE=128
STRENGTH=1.5/math.sqrt(128*9.0)

def rows_iota(n=8):
    return lax.broadcasted_iota(jnp.int32,(n,TILE),0)

def split3(c):
    c1=c.astype(jnp.bfloat16).astype(jnp.float32)
    r=c-c1
    c2=r.astype(jnp.bfloat16).astype(jnp.float32)
    return c1,c2,r-c2

def split2(c):
    c1=c.astype(jnp.bfloat16).astype(jnp.float32)
    return c1,c-c1

def features(s):
    r=rows_iota()
    f=jnp.broadcast_to(s[7:8],(8,TILE)); x=jnp.broadcast_to(s[4:5],(8,TILE)); m=jnp.broadcast_to(s[3:4],(8,TILE))
    c=jnp.where(r==3,f*x,s)
    sq=c*c
    v=sq+pltpu.roll(sq,7,0)+pltpu.roll(sq,6,0)
    w=jnp.where(r==3,sq,v+0.5)
    ones=jnp.where(r==3,f,1.0)
    z=m*jnp.where(r==3,1.0,s)
    z1,z2=split2(z)
    zz=jnp.where(r<4,z1,pltpu.roll(z2,4,0))
    zz=jnp.concatenate([zz,jnp.zeros_like(zz)],0).astype(jnp.bfloat16)
    return split3(c),split3(w),ones,zz,m

def patterns():
    blk=lax.broadcasted_iota(jnp.int32,(96,TILE),0)//8
    row=lax.broadcasted_iota(jnp.int32,(96,TILE),0)%8
    coord=blk<6
    out=[]
    for lo,hi,norm,scale in ((0,3,0,1.0),(4,7,4,1.0),(3,4,3,8.0)):
        a=jnp.where((row>=lo)&(row<hi),-2.0*scale,0.0)
        b=jnp.where(row==norm,scale,0.0)
        out.append(jnp.where(coord,a,b))
    return out

def post(acc,s,m):
    t=acc[:8]
    t=t+pltpu.roll(t,4,0)
    sw=jnp.broadcast_to(t[3:4],(8,TILE))
    return (STRENGTH*m)*(t-s*sw)

def bond(so,sp,fo,fp,pat_ref,word,both):
    (c1,c2,c3),(w1,w2,w3),one,zo,mo=fo
    (d1,d2,d3),(x1,x2,x3),onep,zp,mp=fp
    left=jnp.concatenate([c1,c1,c2,c2,c1,c3,w1,w2,w3,one,one,one],0).astype(jnp.bfloat16)
    base=jnp.concatenate([d1,d2,d1,d2,d3,d1,onep,onep,onep,x1,x2,x3],0).astype(jnp.bfloat16)
    right=jnp.concatenate([base*pat_ref[0],base*pat_ref[1],base*pat_ref[2]],1)
    d=lax.dot_general(left,right,(((0,),(0,)),((),())),preferred_element_type=jnp.float32)
    il=lax.rsqrt(jnp.maximum(d[:,:TILE],1.0))
    iL=lax.rsqrt(d[:,TILE:2*TILE])
    w=(iL-il)*(1.0+d[:,2*TILE:]*(iL*iL))
    if word is not None:
        w=jnp.concatenate([jnp.where((word&(1<<k))!=0,w[8*k:8*k+8],0.0) for k in range(16)],0)
    wh=w.astype(jnp.bfloat16)
    wl=(w-wh.astype(jnp.float32)).astype(jnp.bfloat16)
    nt=(((1,),(1,)),((),()))
    ao=lax.dot_general(zp,wh,nt,preferred_element_type=jnp.float32)+lax.dot_general(zp,wl,nt,preferred_element_type=jnp.float32)
    on_o=post(ao,so,mo)
    if not both: return on_o,None
    ap=jnp.dot(zo,wh,preferred_element_type=jnp.float32)+jnp.dot(zo,wl,preferred_element_type=jnp.float32)
    return on_o,post(ap,sp,mp)

def pair_kernel(n_col,n_row,unroll,own_ref,count_ref,owner_ref,partner_ref,row_ref,col_ref,packed_ref,rowf_ref,colf_ref,pat_ref):
    for k,p in enumerate(patterns()):
        pat_ref[k]=p.astype(jnp.bfloat16)
    rowf_ref[...]=jnp.zeros_like(rowf_ref)
    colf_ref[...]=jnp.zeros_like(colf_ref)
    live=count_ref[0]
    def load(ref,t):
        return ref[pl.ds((t//16)*128+t%16,8,stride=16),:]
    def add(ref,t,val):
        at=pl.ds((t//16)*48+t%16,3,stride=16)
        ref[at,:]=ref[at,:]+val[:3]
    def own_body(i,c):
        base=own_ref[0]*16
        res=[]
        for j in range(unroll):
            t=base+i*unroll+j
            s=load(row_ref,t)
            f=features(s)
            res.append((t,bond(s,s,f,f,pat_ref,None,False)[0]))
        for t,v in res: add(rowf_ref,t,v)
        return c
    lax.fori_loop(0,16//unroll,own_body,0)
    def body(i,c):
        res=[]
        for j in range(unroll):
            slot=i*unroll+j
            o=owner_ref[slot]; p=partner_ref[slot]
            so=load(row_ref,o); sp=load(col_ref,p)
            alive=jnp.where(slot<live,-1,0)
            word=packed_ref[slot]&alive
            a,b=bond(so,sp,features(so),features(sp),pat_ref,word,True)
            res.append((o,p,a,b))
        for o,p,a,b in res:
            add(rowf_ref,o,a); add(colf_ref,p,b)
        return c
    lax.fori_loop(0,(live+unroll-1)//unroll,body,0)

def pair_forces(own,count,owner,partner,row,col,packed,unroll=4):
    n_col=row.shape[0]//128; n_row=col.shape[0]//128
    smem=pl.BlockSpec(memory_space=pltpu.SMEM); vmem=pl.BlockSpec(memory_space=pltpu.VMEM)
    return pl.pallas_call(functools.partial(pair_kernel,n_col,n_row,unroll),
        out_shape=(jax.ShapeDtypeStruct((n_col*48,TILE),jnp.float32),jax.ShapeDtypeStruct((n_row*48,TILE),jnp.float32)),
        in_specs=[smem]*4+[vmem]*3,out_specs=(vmem,vmem),
        scratch_shapes=[pltpu.VMEM((3,96,TILE),jnp.bfloat16)],
        compiler_params=pltpu.CompilerParams(vmem_limit_bytes=48*2**20),
        name="pair_forces")(own,count,owner,partner,row,col,packed)

def pack_kernel(count_ref,bond_ref,broken_ref,out_ref):
    i=pl.program_id(0)
    @pl.when(i*8<count_ref[0])
    def _():
        for j in range(8):
            acc=None
            for k in range(16):
                b=bond_ref[j,8*k:8*k+8,:]; c=broken_ref[j,8*k:8*k+8,:]
                t=(b&(1-c))<<k
                acc=t if acc is None else acc|t
            out_ref[j]=acc

def pack(count,bond_mask,broken):
    n=bond_mask.shape[0]
    def idx(i,cnt): return (jnp.minimum(i,(cnt[0]+7)//8-1),0,0)
    return pl.pallas_call(pack_kernel,
        grid_spec=pltpu.PrefetchScalarGridSpec(num_scalar_prefetch=1,grid=(n//8,),
            in_specs=[pl.BlockSpec((8,TILE,TILE),idx)]*2,out_specs=pl.BlockSpec((8,8,TILE),idx)),
        out_shape=jax.ShapeDtypeStruct((n,8,TILE),jnp.int32),
        compiler_params=pltpu.CompilerParams(vmem_limit_bytes=48*2**20),
        name="pack_bonds")(count,bond_mask,broken)


STEPS=2
TIME_STEP=0.5


def spread(block, axis, n):
    return lax.all_to_all(jnp.broadcast_to(block[None],(n,)+block.shape),axis,0,0,tiled=True)


def gather_sum(parts, axis):
    return jnp.sum(lax.all_to_all(parts,axis,0,0,tiled=True),axis=0)


def per_device(rest_pos, displacement, velocity, accel_prev, material, moduli, pair_owner, pair_partner, pair_count, bond_mask, broken):
    n_row=lax.axis_size("row"); n_col=lax.axis_size("col")
    tiles=material.shape[0]//TILE
    shape=(3,tiles,TILE)
    rest=rest_pos.reshape(shape)-2.0
    u=displacement.reshape(shape); v=velocity.reshape(shape); a=accel_prev.reshape(shape)
    fibrous=material.reshape(1,tiles,TILE).astype(jnp.float32)
    root=jnp.sqrt(moduli)
    root=jnp.where(material.reshape(1,tiles,TILE)==1,root[1],root[0])
    own=lax.axis_index("col").reshape(1).astype(jnp.int32)
    packed=pack(pair_count,bond_mask,broken)
    fixed_row=fixed_col=None
    for step in range(STEPS):
        v=v+0.5*TIME_STEP*a
        u=u+TIME_STEP*v
        if step==0:
            state=jnp.concatenate([rest+u,root,rest,fibrous],0)
            row=spread(state,"col",n_col); col=spread(state,"row",n_row)
        else:
            row=jnp.concatenate([spread(rest+u,"col",n_col),row[:,3:]],1)
            col=jnp.concatenate([spread(rest+u,"row",n_row),col[:,3:]],1)
        rowf,colf=pair_forces(own,pair_count,pair_owner,pair_partner,row.reshape(-1,TILE),col.reshape(-1,TILE),packed,8)
        a=(gather_sum(rowf.reshape((n_col,)+shape),"col")+gather_sum(colf.reshape((n_row,)+shape),"row"))
        v=v+0.5*TIME_STEP*a
    return u.reshape(3,-1),v.reshape(3,-1)


def solution(mesh):
    points=P(None,("row","col")); flat=P(("row","col")); masks=P(("row","col"),None,None)
    return jax.shard_map(per_device,mesh=mesh,in_specs=(points,)*4+(flat,P())+(flat,)*3+(masks,)*2,out_specs=(points,points),check_vma=False)
```

time: 697 us -> 174 us (0.25)
  waiting for transfers between devices: 340 us -> 40.2 us
  other arithmetic: 225 us -> 5.19 us
  local copies, waits for them, and re-layouts: 80 us -> 3.24 us
  Pallas kernels: 0 us -> 39.5 us
  starting transfers between devices: 0.25 us -> 37.8 us
  blocking collectives: 28.4 us -> 46.6 us
  between operations: 14.3 us -> 1.47 us
    psum x4 -> x0, waiting for transfers between devices: 281 us -> none  [the longest x2 173 us: reduce_forces(): row_whole = lax.psum(row_force, 'col')]
    reduce_sum x36 -> x4, other arithmetic: 126 us -> 0.09 us  [gather_sum(): return jnp.sum(lax.all_to_all(parts, axis, 0, 0, tiled=True), axis=0)]
    gather x64 -> x0, local copies, waits for them, and re-layouts: 74.5 us -> none  [the longest x32 56.8 us: add_block(): owners = jnp.take(row_block, owner_ids, axis=1)]
    all_gather x2 -> x0, waiting for transfers between devices: 59.4 us -> none  [ghost_blocks(): row_block = lax.all_gather(state_rows, 'col', axis=1, tiled=True)]
    scatter-add x64 -> x0, other arithmetic: 49.8 us -> none  [the longest x32 24.9 us: add_block(): forces[1].at[:, partner_ids].add(on_partner)]
    all_to_all x0 -> x4, blocking collectives: none -> 46.6 us  [the longest x2 24.8 us: spread(): lax.all_to_all(jnp.broadcast_to(block[None], (n,) + block.shape), axis, 0...]
    all_to_all x0 -> x4, waiting for transfers between devices: none -> 40.2 us  [the longest x2 20.6 us: spread(): lax.all_to_all(jnp.broadcast_to(block[None], (n,) + block.shape), axis, 0...]
    pallas_call x0 -> x3, Pallas kernels: none -> 39.5 us  [the longest x2 33.7 us: pair_forces(): pl.pallas_call(functools.partial(pair_kernel, n_col, n_row, unroll), out_...]
  transfers between devices with their start and end apart: 6 -> 4, of which waited for: 6 -> 4; matrix products, arithmetic and copies ran while one was open for 1% -> 0% of each run, Pallas kernels for 0% -> 3%
where the time goes in v1:
time: 174 us
  blocking collectives  46.6 us (27%)
  waiting for transfers between devices  40.2 us (23%)
  Pallas kernels  39.5 us (23%)
  starting transfers between devices  37.8 us (22%)
  other arithmetic  5.19 us (3%)
  local copies, waits for them, and re-layouts  3.24 us (2%)
    pallas_call x2, Pallas kernels, pair_forces(): pl.pallas_call(functools.partial(pair_kernel, n_col, n_row, unroll), out_...  33.7 us
    all_to_all x2, starting transfers between devices, gather_sum(): return jnp.sum(lax.all_to_all(parts, axis, 0, 0, tiled=True), axis=0)  27.3 us
    all_to_all x2, blocking collectives, spread(): lax.all_to_all(jnp.broadcast_to(block[None], (n,) + block.shape), axis, 0...  24.8 us
    all_to_all x2, blocking collectives, gather_sum(): return jnp.sum(lax.all_to_all(parts, axis, 0, 0, tiled=True), axis=0)  21.8 us
    all_to_all x2, waiting for transfers between devices, spread(): lax.all_to_all(jnp.broadcast_to(block[None], (n,) + block.shape), axis, 0...  20.6 us
    all_to_all x2, waiting for transfers between devices, gather_sum(): return jnp.sum(lax.all_to_all(parts, axis, 0, 0, tiled=True), axis=0)  19.6 us
    all_to_all x2, starting transfers between devices, spread(): lax.all_to_all(jnp.broadcast_to(block[None], (n,) + block.shape), axis, 0...  10.6 us
    pallas_call x1, Pallas kernels, pack(): pl.pallas_call(pack_kernel, grid_spec=pltpu.PrefetchScalarGridSpec(num_sc...  5.76 us
  transfers between devices with their start and end apart: 4, of which 4 were waited for; matrix products, arithmetic and copies ran while one was open for 0% of the time, Pallas kernels for 3%

profile of v1, /device:TPU:0, one launch (start us, length us, event | category | flops | bytes accessed | tf_op | source)
XLA Modules:
  0.0 174.1 jit_solution(5920690311616196753)
XLA Ops:
  0.6 0.7 sqrt.3
  1.3 0.6 fusion.7
  1.9 0.7 convert_bitcast_fusion
  2.6 2.0 %select_bitcast_fusion = f32[1,16,128]{2,1,0:T(8,128)S(1)} fusion(s32[2048]{0:T(1024)} %param.15, f32[]{:T(128)} %bitcast.2, f32[]{:T(128)} %bitcast.1), kind=kLoop, calls=%fused_computation.20 | loop fusion | flops 4096 | bytes 16392 | tf_op jit(solution)/shard_map/jit(_where)/select_n | solution.py:166
  4.6 0.8 add_bitcast_fusion
  5.4 0.8 fusion.4
  6.2 15.6 %all_to_all.40 = f32[8,8,16,128]{3,2,1,0:T(8,128)S(1)} all-to-all(f32[8,8,16,128]{3,2,1,0:T(8,128)S(1)} %broadcast_in_dim.19), channel_id=1, replica_groups=mesh['row'=8,'col'=16] {'row'}, dimensions={0} | all-to-all | bytes 1048576 | tf_op jit(solution)/shard_map/all_to_all | solution.py:151
  21.8 1.1 broadcast_in_dim.18
  22.9 7.0 %all-to-all-start = ((f32[16,8,16,128]{3,2,1,0:T(8,128)}), f32[16,8,16,128]{3,2,1,0:T(8,128)S(1)}, u32[]{:S(2)}, u32[]{:S(2)}) async-start(f32[16,8,16,128]{3,2,1,0:T(8,128)} %broadcast_in_dim.18), calls=%async_computation | async-start | bytes 2097152 | tf_op jit(solution)/shard_map/all_to_all | solution.py:151
  30.6 0.0 copy-start
  30.6 0.0 copy-start.1
  30.6 0.0 copy-start.2
  30.6 5.8 %pack_bonds.1.packed_ref = s32[128,8,128]{2,1,0:T(8,128)S(1)} custom-call(s32[1]{0:T(128)S(6)} %copy.37.count_ref, s32[128,128,128]{2,1,0:T(8,128)} %bond_ref.1, s32[128,128,128]{2,1,0:T(8,128)} %broken_ref.1), custom_call_target="tpu_custom_call" | custom-call | tf_op jit(solution)/shard_map/pack_bonds/pallas_call | solution.py:138
  36.4 0.0 copy-start.3
  36.4 0.0 copy-start.4
  36.4 10.7 %all-to-all-done = f32[16,8,16,128]{3,2,1,0:T(8,128)S(1)} async-done(((f32[16,8,16,128]{3,2,1,0:T(8,128)}), f32[16,8,16,128]{3,2,1,0:T(8,128)S(1)}, u32[]{:S(2)}, u32[]{:S(2)}) %all-to-all-start) | async-done | bytes 1048608 | tf_op jit(solution)/shard_map/all_to_all | solution.py:151
  47.1 0.0 copy-done
  47.1 0.0 copy-done.1
  47.1 16.8 %pair_forces.2 = (f32[768,128]{1,0:T(8,128)}, f32[384,128]{1,0:T(8,128)S(1)}) custom-call(s32[1]{0:T(128)} %bitcast.own_ref, s32[1]{0:T(128)S(6)} %copy.37.count_ref, s32[128]{0:T(128)S(1)} %copy-done, s32[128]{0:T(128)S(1)} %copy-done.1, f32[2048,128]{1,0:T(8,128)S(1)} %bitcast.50, f32[1024,128]{1,0:T(8,128)S(1)} %bitcast.52, ...), custom_call_target="tpu_custom_call" | custom-call | tf_op jit(solution)/shard_map/pair_forces/pallas_call | solution.py:116
  64.0 10.9 %all_to_all.41 = f32[8,3,16,128]{3,2,1,0:T(8,128)S(1)} all-to-all(f32[8,3,16,128]{3,2,1,0:T(8,128)S(1)} %bitcast.55), channel_id=1, replica_groups=mesh['row'=8,'col'=16] {'row'}, dimensions={0} | all-to-all | bytes 393216 | tf_op jit(solution)/shard_map/all_to_all | solution.py:155
  74.9 13.1 %all-to-all-start.2 = ((f32[16,3,16,128]{3,2,1,0:T(8,128)}), f32[16,3,16,128]{3,2,1,0:T(8,128)S(1)}, u32[]{:S(2)}, u32[]{:S(2)}) async-start(f32[16,3,16,128]{3,2,1,0:T(8,128)} %bitcast.7), calls=%async_computation.2 | async-start | bytes 786432 | tf_op jit(solution)/shard_map/all_to_all | solution.py:155
  88.0 9.8 %all-to-all-done.2 = f32[16,3,16,128]{3,2,1,0:T(8,128)S(1)} async-done(((f32[16,3,16,128]{3,2,1,0:T(8,128)}), f32[16,3,16,128]{3,2,1,0:T(8,128)S(1)}, u32[]{:S(2)}, u32[]{:S(2)}) %all-to-all-start.2) | async-done | bytes 393248 | tf_op jit(solution)/shard_map/all_to_all | solution.py:155
  97.8 0.0 copy-done.2
  97.9 9.2 %all_to_all.42 = f32[8,3,16,128]{3,2,1,0:T(8,128)S(1)} all-to-all(f32[8,3,16,128]{3,2,1,0:T(8,128)S(1)} %broadcast_in_dim.37), channel_id=1, replica_groups=mesh['row'=8,'col'=16] {'row'}, dimensions={0} | all-to-all | bytes 393216 | tf_op jit(solution)/shard_map/all_to_all | solution.py:151
  107.1 0.8 broadcast_in_dim.36
  107.9 3.6 %all-to-all-start.4 = ((f32[16,3,16,128]{3,2,1,0:T(8,128)}), f32[16,3,16,128]{3,2,1,0:T(8,128)S(1)}, u32[]{:S(2)}, u32[]{:S(2)}) async-start(f32[16,3,16,128]{3,2,1,0:T(8,128)} %broadcast_in_dim.36), calls=%async_computation.4 | async-start | bytes 786432 | tf_op jit(solution)/shard_map/all_to_all | solution.py:151
  111.6 9.9 %all-to-all-done.4 = f32[16,3,16,128]{3,2,1,0:T(8,128)S(1)} async-done(((f32[16,3,16,128]{3,2,1,0:T(8,128)}), f32[16,3,16,128]{3,2,1,0:T(8,128)S(1)}, u32[]{:S(2)}, u32[]{:S(2)}) %all-to-all-start.4) | async-done | bytes 393248 | tf_op jit(solution)/shard_map/all_to_all | solution.py:151
  121.5 0.1 pad_maximum_fusion
  121.6 16.9 %pair_forces.3 = (f32[768,128]{1,0:T(8,128)}, f32[384,128]{1,0:T(8,128)S(1)}) custom-call(s32[1]{0:T(128)} %bitcast.own_ref, s32[1]{0:T(128)S(6)} %copy.37.count_ref, s32[128]{0:T(128)S(1)} %copy-done, s32[128]{0:T(128)S(1)} %copy-done.1, f32[2048,128]{1,0:T(8,128)S(1)} %bitcast.51, f32[1024,128]{1,0:T(8,128)S(1)} %bitcast.53, ...), custom_call_target="tpu_custom_call" | custom-call | tf_op jit(solution)/shard_map/pair_forces/pallas_call | solution.py:116
  138.4 10.9 %all_to_all.43 = f32[8,3,16,128]{3,2,1,0:T(8,128)S(1)} all-to-all(f32[8,3,16,128]{3,2,1,0:T(8,128)S(1)} %bitcast.54), channel_id=1, replica_groups=mesh['row'=8,'col'=16] {'row'}, dimensions={0} | all-to-all | bytes 393216 | tf_op jit(solution)/shard_map/all_to_all | solution.py:155
  149.4 14.2 %all-to-all-start.6 = ((f32[16,3,16,128]{3,2,1,0:T(8,128)}), f32[16,3,16,128]{3,2,1,0:T(8,128)S(1)}, u32[]{:S(2)}, u32[]{:S(2)}) async-start(f32[16,3,16,128]{3,2,1,0:T(8,128)} %bitcast.11), calls=%async_computation.6 | async-start | bytes 786432 | tf_op jit(solution)/shard_map/all_to_all | solution.py:155
  163.5 9.8 %all-to-all-done.6 = f32[16,3,16,128]{3,2,1,0:T(8,128)S(1)} async-done(((f32[16,3,16,128]{3,2,1,0:T(8,128)}), f32[16,3,16,128]{3,2,1,0:T(8,128)S(1)}, u32[]{:S(2)}, u32[]{:S(2)}) %all-to-all-start.6) | async-done | bytes 393248 | tf_op jit(solution)/shard_map/all_to_all | solution.py:155
  173.4 0.0 copy-done.3
  173.4 0.0 copy-done.4
  173.4 0.7 bitcast_add_fusion
  (12 shorter events, 0.3 us)
Async XLA Ops:
  22.9 24.2 %all-to-all-start = ((f32[16,8,16,128]{3,2,1,0:T(8,128)}), f32[16,8,16,128]{3,2,1,0:T(8,128)S(1)}, u32[]{:S(2)}, u32[]{:S(2)}) async-start(f32[16,8,16,128]{3,2,1,0:T(8,128)} %broadcast_in_dim.18), calls=%async_computation | async-start | bytes 2097152 | tf_op jit(solution)/shard_map/all_to_all | solution.py:151
  30.6 16.6 %copy-start = (s32[128]{0:T(128)S(1)}, s32[128]{0:T(128)}, u32[]{:S(2)}) copy-start(s32[128]{0:T(128)} %owner_ref.3) | copy-start | bytes 1540
  30.6 16.5 %copy-start.1 = (s32[128]{0:T(128)S(1)}, s32[128]{0:T(128)}, u32[]{:S(2)}) copy-start(s32[128]{0:T(128)} %partner_ref.3) | copy-start | bytes 1540
  30.6 67.2 %copy-start.2 = (f32[3,2048]{1,0:T(4,128)S(1)}, f32[3,2048]{1,0:T(4,128)}, u32[]{:S(2)}) copy-start(f32[3,2048]{1,0:T(4,128)} %param.12) | copy-start | bytes 73732
  36.4 137.0 %copy-start.3 = (f32[3,2048]{1,0:T(4,128)S(1)}, f32[3,2048]{1,0:T(4,128)}, u32[]{:S(2)}) copy-start(f32[3,2048]{1,0:T(4,128)} %param.13) | copy-start | bytes 73732
  36.4 137.0 %copy-start.4 = (f32[3,2048]{1,0:T(4,128)S(1)}, f32[3,2048]{1,0:T(4,128)}, u32[]{:S(2)}) copy-start(f32[3,2048]{1,0:T(4,128)} %param.14) | copy-start | bytes 73732
  74.9 22.9 %all-to-all-start.2 = ((f32[16,3,16,128]{3,2,1,0:T(8,128)}), f32[16,3,16,128]{3,2,1,0:T(8,128)S(1)}, u32[]{:S(2)}, u32[]{:S(2)}) async-start(f32[16,3,16,128]{3,2,1,0:T(8,128)} %bitcast.7), calls=%async_computation.2 | async-start | bytes 786432 | tf_op jit(solution)/shard_map/all_to_all | solution.py:155
  107.9 13.6 %all-to-all-start.4 = ((f32[16,3,16,128]{3,2,1,0:T(8,128)}), f32[16,3,16,128]{3,2,1,0:T(8,128)S(1)}, u32[]{:S(2)}, u32[]{:S(2)}) async-start(f32[16,3,16,128]{3,2,1,0:T(8,128)} %broadcast_in_dim.36), calls=%async_computation.4 | async-start | bytes 786432 | tf_op jit(solution)/shard_map/all_to_all | solution.py:151
  149.4 24.0 %all-to-all-start.6 = ((f32[16,3,16,128]{3,2,1,0:T(8,128)}), f32[16,3,16,128]{3,2,1,0:T(8,128)S(1)}, u32[]{:S(2)}, u32[]{:S(2)}) async-start(f32[16,3,16,128]{3,2,1,0:T(8,128)} %bitcast.11), calls=%async_computation.6 | async-start | bytes 786432 | tf_op jit(solution)/shard_map/all_to_all | solution.py:155

commit v2 on v1

v2 whole, which is shorter than its diff:
```python
import functools
import math

import jax
import jax.numpy as jnp
from jax import lax
from jax.experimental import pallas as pl
from jax.experimental.pallas import tpu as pltpu
from jax.sharding import PartitionSpec as P

TILE = 128
TILE_DEV = 16
PAIRS_DEV = 128
STEPS = 2
TIME_STEP = 0.5
CENTRE = 2.0
STRENGTH = 1.5 / math.sqrt(TILE * (1.0 + PAIRS_DEV / TILE_DEV))
UNROLL = 16
CORES = 2
PACK = 16
LIMIT = 48 * 2**20
VMEM = pl.BlockSpec(memory_space=pltpu.VMEM)
SMEM = pl.BlockSpec(memory_space=pltpu.SMEM)


def f32(*shape):
    return jax.ShapeDtypeStruct(shape, jnp.float32)


def rows_iota(n=8):
    return lax.broadcasted_iota(jnp.int32,(n,TILE),0)

def halves(c):
    c1=c.astype(jnp.bfloat16).astype(jnp.float32)
    return c1,(c-c1).astype(jnp.bfloat16).astype(jnp.float32)

def thirds(c):
    c1,c2=halves(c)
    return c1,c2,(c-c1)-c2

def row_of(s,k):
    return jnp.broadcast_to(s[k:k+1],(8,TILE))

def features(s,owner,alive=None):
    r=rows_iota()
    f=row_of(s,7); m=row_of(s,3)
    if alive is not None:
        m=m*alive
    c1,c2=halves(jnp.where(r==3,f*row_of(s,4),s))
    c=c1+c2
    sq=c*c
    w=jnp.where(r==3,sq,sq+pltpu.roll(sq,7,0)+pltpu.roll(sq,6,0)+0.5)
    z1,z2=halves(m*jnp.where(r==3,1.0,s))
    z=jnp.where(r<4,z1,pltpu.roll(z2,4,0))
    z=jnp.concatenate([z,jnp.zeros_like(z)],0).astype(jnp.bfloat16)
    if owner:
        ones=jnp.where(r==5,f,1.0)
        n=[jnp.where((r==0)|(r==3)|(r==4),t,ones) for t in thirds(w)]
        x=[c1,c1,c2,c2]+n+[jnp.zeros_like(ones)]
    else:
        ones=jnp.where(r==3,f,1.0)
        n=[jnp.where((r==2)|(r==5)|(r==6),t,ones) for t in thirds(pltpu.roll(w,2,0))]
        x=[c1,c2,c1,c2]+n+[jnp.zeros_like(ones)]
    return jnp.concatenate(x,0).astype(jnp.bfloat16),z,m

def patterns():
    row=lax.broadcasted_iota(jnp.int32,(64,TILE),0)
    coord=row<32; spare=row>=56
    row=row%8
    def pick(lo,hi,n1,n2,scale):
        c=jnp.where((row>=lo)&(row<hi),-2.0*scale,0.0)
        n=jnp.where((row==n1)|(row==n2),scale,0.0)
        return jnp.where(spare,0.0,jnp.where(coord,c,n))
    now=pick(0,3,0,2,1.0); rest=pick(4,7,4,6,1.0)
    return now,rest,rest+pick(3,4,3,5,8.0)

def post(acc,s,m):
    t=acc[:8,:TILE]+acc[:8,TILE:]
    t=t+pltpu.roll(t,4,0)
    return (STRENGTH*m)*(t-s*row_of(t,3))

def lengths(left,base,pat_ref):
    right=jnp.concatenate([base*pat_ref[0],base*pat_ref[1],base*pat_ref[2]],1)
    return lax.dot_general(left,right,(((0,),(0,)),((),())),preferred_element_type=jnp.float32)

def weights(d,mask):
    il=lax.rsqrt(jnp.maximum(d[:,:TILE],1.0))
    iL=lax.rsqrt(d[:,TILE:2*TILE])
    w=(iL-il)*(d[:,2*TILE:]*(iL*iL))
    wh=w.astype(jnp.bfloat16)
    wl=(w-wh.astype(jnp.float32)).astype(jnp.bfloat16)
    if mask is not None:
        wh=wh*mask; wl=wl*mask
    return wh,wl

def sum_owner(z,w):
    return lax.dot_general(z,jnp.concatenate(w,0),(((1,),(1,)),((),())),preferred_element_type=jnp.float32)

def sum_partner(z,w):
    return jnp.dot(z,jnp.concatenate(w,1),preferred_element_type=jnp.float32)

def pack_kernel(count_ref,bond_ref,broken_ref,out_ref):
    i=pl.program_id(0)
    @pl.when(i*PACK<count_ref[0])
    def _():
        out_ref[...]=(bond_ref[...]*(1-broken_ref[...])).astype(jnp.float32).astype(jnp.bfloat16)

def pack(count,bond_mask,broken):
    n=bond_mask.shape[0]
    def idx(i,cnt): return (jnp.minimum(i,(cnt[0]+PACK-1)//PACK-1),0,0)
    return pl.pallas_call(pack_kernel,
        grid_spec=pltpu.PrefetchScalarGridSpec(num_scalar_prefetch=1,grid=(n//PACK,),
            in_specs=[pl.BlockSpec((PACK,TILE,TILE),idx)]*2,out_specs=pl.BlockSpec((PACK,TILE,TILE),idx)),
        out_shape=jax.ShapeDtypeStruct((n,TILE,TILE),jnp.bfloat16),
        compiler_params=pltpu.CompilerParams(vmem_limit_bytes=LIMIT),
        name="pack_bonds")(count,bond_mask,broken)

def pair_kernel(n_z, fresh, *refs):
    count_ref, owner_ref, partner_ref, mask_ref, row_ref = refs[:5]
    col_refs = refs[5:5 + n_z]
    at = 5 + n_z
    now_row_ref, now_col_refs = None, None
    if not fresh:
        now_row_ref = refs[at]
        now_col_refs = refs[at + 1:at + 1 + n_z]
        at += 1 + n_z
    rowf_ref, mine_ref, sibling_ref, pat_ref, rows_ref, cols_ref, colf_ref = refs[at:]
    n_col = row_ref.shape[0]
    full = 8 * TILE_DEV
    part = 3 * TILE_DEV
    at_row = lax.axis_index("row")
    z, core = at_row // CORES, at_row % CORES
    for k, p in enumerate(patterns()):
        pat_ref[k] = p.astype(jnp.bfloat16)
    rowf_ref[...] = jnp.zeros_like(rowf_ref)
    colf_ref[...] = jnp.zeros_like(colf_ref)
    for c in range(n_col):
        rows_ref[c * full:(c + 1) * full] = row_ref[c].reshape(full, TILE)
        if not fresh:
            rows_ref[c * full:c * full + part] = now_row_ref[c].reshape(part, TILE)
    for d in range(n_z):
        src = (z + n_z - d) % n_z
        for j in range(CORES):
            r = src * CORES + (core if j == 0 else 1 - core)
            start = pl.multiple_of(r * full, full)
            cols_ref[pl.ds(start, full)] = col_refs[d][j].reshape(full, TILE)
            if not fresh:
                cols_ref[pl.ds(start, part)] = now_col_refs[d][j].reshape(part, TILE)
    live = count_ref[0]

    def load(ref, t):
        return ref[pl.ds((t // TILE_DEV) * full + t % TILE_DEV, 8, stride=TILE_DEV), :]

    def add(ref, t, val):
        where = pl.ds((t // TILE_DEV) * part + t % TILE_DEV, 3, stride=TILE_DEV)
        ref[where, :] = ref[where, :] + val[:3]

    def run(slots, masks, both):
        d = [lengths(fo[0], fp[0], pat_ref) for _, _, _, _, fo, fp in slots]
        w = [weights(x, m) for x, m in zip(d, masks)]
        ao = [sum_owner(q[5][1], x) for q, x in zip(slots, w)]
        ap = [sum_partner(q[4][1], x) for q, x in zip(slots, w)] if both else None
        for j, (o, p, so, sp, fo, fp) in enumerate(slots):
            add(rowf_ref, o, post(ao[j], so, fo[2]))
            if both:
                add(colf_ref, p, post(ap[j], sp, fp[2]))

    own = []
    for j in range(TILE_DEV):
        t = lax.axis_index("col") * TILE_DEV + j
        s = load(rows_ref, t)
        own.append((t, t, s, s, features(s, True), features(s, False)))
    run(own, [None] * TILE_DEV, False)

    def body(i, carry):
        slots = []
        masks = []
        for j in range(UNROLL):
            slot = i * UNROLL + j
            o = owner_ref[slot]
            p = partner_ref[slot]
            so = load(rows_ref, o)
            sp = load(cols_ref, p)
            alive = jnp.where(slot < live, 1.0, 0.0)
            slots.append((o, p, so, sp, features(so, True, alive), features(sp, False, alive)))
            masks.append(mask_ref[slot])
        run(slots, masks, True)
        return carry

    lax.fori_loop(0, (live + UNROLL - 1) // UNROLL, body, 0)
    for i in range(n_z):
        for ref, c in ((mine_ref, core), (sibling_ref, 1 - core)):
            start = pl.multiple_of((i * CORES + c) * part, part)
            ref[i] = colf_ref[pl.ds(start, part)].reshape(3, TILE_DEV, TILE)


def pair_forces(count, owner, partner, masks, row, cols, now_row=None, now_cols=()):
    n_col, n_z = row.shape[0], len(cols)
    fresh = now_row is None
    more = () if fresh else (now_row, *now_cols)
    shares = f32(n_z, 3, TILE_DEV, TILE)
    return pl.pallas_call(
        functools.partial(pair_kernel, n_z, fresh),
        out_shape=(f32(n_col * 3 * TILE_DEV, TILE), shares, shares),
        in_specs=[SMEM] * 3 + [VMEM] * (2 + n_z + len(more)),
        out_specs=(VMEM,) * 3,
        scratch_shapes=[
            pltpu.VMEM((3, 64, TILE), jnp.bfloat16),
            pltpu.VMEM((n_col * 8 * TILE_DEV, TILE), jnp.float32),
            pltpu.VMEM((n_z * CORES * 8 * TILE_DEV, TILE), jnp.float32),
            pltpu.VMEM((n_z * CORES * 3 * TILE_DEV, TILE), jnp.float32),
        ],
        compiler_params=pltpu.CompilerParams(vmem_limit_bytes=LIMIT),
        name="pair_forces",
    )(count, owner, partner, masks, row, *cols, *more)


def start_kernel(moduli_ref, material_ref, rest_ref, disp_ref, vel_ref, acc_ref, spread_ref, state_ref, u_ref, v_ref):
    for c in range(3):
        for t in range(TILE_DEV):
            lanes = pl.ds(t * TILE, TILE)
            v = vel_ref[c:c + 1, lanes] + 0.5 * TIME_STEP * acc_ref[c:c + 1, lanes]
            u = disp_ref[c:c + 1, lanes] + TIME_STEP * v
            x = rest_ref[c:c + 1, lanes] - CENTRE
            v_ref[c, t:t + 1, :] = v
            u_ref[c, t:t + 1, :] = u
            state_ref[c, t:t + 1, :] = x + u
            state_ref[4 + c, t:t + 1, :] = x
    fibre = material_ref[...] == 1
    modulus = jnp.where(fibre, moduli_ref[1], moduli_ref[0])
    state_ref[3] = jnp.sqrt(modulus)
    state_ref[7] = jnp.where(fibre, 1.0, 0.0)
    for i in range(spread_ref.shape[0]):
        spread_ref[i] = state_ref[...]


def start(n_col, moduli, material, rest, disp, vel, acc):
    block = (3, TILE_DEV, TILE)
    return pl.pallas_call(
        start_kernel,
        out_shape=(f32(n_col, 8, TILE_DEV, TILE), f32(8, TILE_DEV, TILE), f32(*block), f32(*block)),
        in_specs=[SMEM] + [VMEM] * 5,
        out_specs=(VMEM,) * 4,
        name="first_half_step",
    )(moduli, material, rest, disp, vel, acc)


def share_kernel(mine_ref, other_ref, *out_refs):
    n_z = len(out_refs)
    z = lax.axis_index("row") // CORES
    for d, out_ref in enumerate(out_refs):
        at = (z + d) % n_z
        out_ref[...] = mine_ref[at] + other_ref[at]


def shares(mine, other):
    n_z = mine.shape[0]
    return pl.pallas_call(
        share_kernel,
        out_shape=(f32(*mine.shape[1:]),) * n_z,
        in_specs=[VMEM] * 2,
        out_specs=(VMEM,) * n_z,
        name="column_shares",
    )(mine, other)


def total(row_ref, col_refs):
    force = row_ref[0]
    for i in range(1, row_ref.shape[0]):
        force = force + row_ref[i]
    for ref in col_refs:
        force = force + ref[...]
    return force


def step_kernel(n_z, row_ref, *refs):
    col_refs = refs[:n_z]
    state_ref, u_ref, v_ref, spread_ref, now_ref, new_u_ref, new_v_ref = refs[n_z:]
    force = total(row_ref, col_refs)
    v = v_ref[...] + TIME_STEP * force
    u = u_ref[...] + TIME_STEP * v
    now = state_ref[4:7] + u
    new_u_ref[...] = u
    new_v_ref[...] = v
    now_ref[...] = now
    for i in range(spread_ref.shape[0]):
        spread_ref[i] = now


def next_step(row, cols, state, u, v):
    return pl.pallas_call(
        functools.partial(step_kernel, len(cols)),
        out_shape=(f32(*row.shape),) + (f32(*u.shape),) * 3,
        in_specs=[VMEM] * (4 + len(cols)),
        out_specs=(VMEM,) * 4,
        name="next_step",
    )(row, *cols, state, u, v)


def last_kernel(n_z, row_ref, *refs):
    col_refs = refs[:n_z]
    u_ref, v_ref, disp_ref, vel_ref = refs[n_z:]
    v = v_ref[...] + 0.5 * TIME_STEP * total(row_ref, col_refs)
    for c in range(3):
        for t in range(TILE_DEV):
            lanes = pl.ds(t * TILE, TILE)
            disp_ref[c:c + 1, lanes] = u_ref[c, t:t + 1, :]
            vel_ref[c:c + 1, lanes] = v[c, t:t + 1, :]


def last_step(row, cols, u, v):
    points = f32(3, TILE_DEV * TILE)
    return pl.pallas_call(
        functools.partial(last_kernel, len(cols)),
        out_shape=(points, points),
        in_specs=[VMEM] * (3 + len(cols)),
        out_specs=(VMEM,) * 2,
        name="last_half_step",
    )(row, *cols, u, v)


def to_sibling(x, n_row):
    return lax.ppermute(x, "row", [(i, i ^ 1) for i in range(n_row)])


def along_z(x, d, n_row):
    n_z = n_row // CORES
    return lax.ppermute(x, "row", [(i, (i // CORES + d) % n_z * CORES + i % CORES) for i in range(n_row)])


def swap(x):
    return lax.all_to_all(x, "col", 0, 0, tiled=True)


def column_gather(block, n_row):
    both = jnp.stack([block, to_sibling(block, n_row)])
    return [both] + [along_z(both, d, n_row) for d in range(1, n_row // CORES)]


def column_sum(mine, sibling, n_row):
    parts = shares(mine, to_sibling(sibling, n_row))
    return [parts[0]] + [along_z(parts[d], d, n_row) for d in range(1, n_row // CORES)]


def per_device(
    rest_pos, displacement, velocity, accel_prev, material, moduli, pair_owner, pair_partner, pair_count, bond_mask, broken
):
    n_row, n_col = lax.axis_size("row"), lax.axis_size("col")
    spread, state, u, v = start(
        n_col, moduli, material.reshape(TILE_DEV, TILE), rest_pos, displacement, velocity, accel_prev
    )
    row = swap(spread)
    cols = column_gather(state, n_row)
    masks = pack(pair_count, bond_mask, broken)
    now = ()
    for step in range(STEPS):
        rowf, mine, sibling = pair_forces(pair_count, pair_owner, pair_partner, masks, row, cols, *now)
        row_part = swap(rowf.reshape(n_col, 3, TILE_DEV, TILE))
        col_part = column_sum(mine, sibling, n_row)
        if step < STEPS - 1:
            spread, block, u, v = next_step(row_part, col_part, state, u, v)
            now = (swap(spread), column_gather(block, n_row))
    return last_step(row_part, col_part, u, v)


def solution(mesh):
    points, flat, masks = P(None, ("row", "col")), P(("row", "col")), P(("row", "col"), None, None)
    return jax.shard_map(
        per_device,
        mesh=mesh,
        in_specs=(points,) * 4 + (flat, P()) + (flat,) * 3 + (masks,) * 2,
        out_specs=(points, points),
        check_vma=False,
    )
```

time: 174 us -> 106 us (0.61); the launches traced: 174 us -> 104 us
  blocking collectives: 46.6 us -> 0 us
  waiting for transfers between devices: 40.2 us -> 18.7 us
  Pallas kernels: 39.5 us -> 23.8 us
  starting transfers between devices: 37.8 us -> 52.5 us
  other arithmetic: 5.19 us -> 1.59 us
  local copies, waits for them, and re-layouts: 3.24 us -> 6.02 us
    all_to_all x4 -> x0, blocking collectives: 46.6 us -> none  [the longest x2 24.8 us: spread(): lax.all_to_all(jnp.broadcast_to(block[None], (n,) + block.shape), axis, 0...]
    all_to_all x4, waiting for transfers between devices: 40.2 us -> 1.85 us  [swap(): return lax.all_to_all(x, 'col', 0, 0, tiled=True)]
    ppermute x0 -> x16, starting transfers between devices: none -> 22.3 us  [the longest x12 22 us: along_z(): lax.ppermute(x, 'row', [(i, (i // CORES + d) % n_z * CORES + i % CORES) f...]
    ppermute x0 -> x16, waiting for transfers between devices: none -> 16.8 us  [the longest x12 11.4 us: along_z(): lax.ppermute(x, 'row', [(i, (i // CORES + d) % n_z * CORES + i % CORES) f...]
    pallas_call x2 -> x7, Pallas kernels: 33.7 us -> 21.2 us  [the longest x2 12.3 us: pair_forces(): pl.pallas_call(functools.partial(pair_kernel, n_z, fresh), out_shape=(f32...]
    all_to_all x4, starting transfers between devices: 37.8 us -> 30.1 us  [swap(): return lax.all_to_all(x, 'col', 0, 0, tiled=True)]
    unnamed x10 -> x30, local copies, waits for them, and re-layouts: 0.03 us -> 6.02 us
    pallas_call x1, Pallas kernels: 5.76 us -> 2.62 us  [pack(): pl.pallas_call(pack_kernel, grid_spec=pltpu.PrefetchScalarGridSpec(num_sc...]
  transfers between devices with their start and end apart: 4 -> 20, of which waited for: 4 -> 14; matrix products, arithmetic and copies ran while one was open for 0% -> 2% of each run, Pallas kernels for 3% -> 6%
where the time goes in v2:
time: 106 us; the launch traced here: 104 us
  starting transfers between devices  52.5 us (50%)
  Pallas kernels  23.8 us (22%)
  waiting for transfers between devices  18.7 us (18%)
  local copies, waits for them, and re-layouts  6.02 us (6%)
  other arithmetic  1.59 us (2%)
  between operations  1.45 us (1%)
    all_to_all x4, starting transfers between devices, swap(): return lax.all_to_all(x, 'col', 0, 0, tiled=True)  30.1 us
    ppermute x12, starting transfers between devices, along_z(): lax.ppermute(x, 'row', [(i, (i // CORES + d) % n_z * CORES + i % CORES) f...  22 us
    pallas_call x2, Pallas kernels, pair_forces(): pl.pallas_call(functools.partial(pair_kernel, n_z, fresh), out_shape=(f32...  12.3 us
    ppermute x12, waiting for transfers between devices, along_z(): lax.ppermute(x, 'row', [(i, (i // CORES + d) % n_z * CORES + i % CORES) f...  11.4 us
    unnamed x30, local copies, waits for them, and re-layouts  6.02 us
    ppermute x4, waiting for transfers between devices, to_sibling(): return lax.ppermute(x, 'row', [(i, i ^ 1) for i in range(n_row)])  5.42 us
    pallas_call x2, Pallas kernels, shares(): pl.pallas_call(share_kernel, out_shape=(f32(*mine.shape[1:]),) * n_z, in_...  3.19 us
    pallas_call x1, Pallas kernels, pack(): pl.pallas_call(pack_kernel, grid_spec=pltpu.PrefetchScalarGridSpec(num_sc...  2.62 us
  transfers between devices with their start and end apart: 20, of which 14 were waited for; matrix products, arithmetic and copies ran while one was open for 2% of the time, Pallas kernels for 6%

profile of v2, /device:TPU:0, one launch (start us, length us, event | category | flops | bytes accessed | tf_op | source)
XLA Modules:
  0.0 104.0 jit_solution(12153606569471055028)
XLA Ops:
  0.6 2.0 %first_half_step.1 = (f32[16,8,16,128]{3,2,1,0:T(8,128)}, f32[8,16,128]{2,1,0:T(8,128)}, f32[3,16,128]{2,1,0:T(8,128)}, f32[3,16,128]{2,1,0:T(8,128)}) custom-call(f32[2]{0:T(128)} %moduli_ref.1, s32[16,128]{1,0:T(8,128)} %bitcast.11, f32[3,2048]{1,0:T(4,128)} %rest_ref.1, f32[3,2048]{1,0:T(4,128)} %disp_ref.1, f32[3,2048]{1,0:T(4,128)} %vel_ref.1, ...), custom_call_target="tpu_custom_call" | custom-call | tf_op jit(solution)/shard_map/first_half_step/pallas_call | solution.py:239
  2.7 7.1 %all-to-all-start = ((f32[16,8,16,128]{3,2,1,0:T(8,128)}), f32[16,8,16,128]{3,2,1,0:T(8,128)S(1)}, u32[]{:S(2)}, u32[]{:S(2)}) async-start(f32[16,8,16,128]{3,2,1,0:T(8,128)} %get-tuple-element.24), calls=%async_computation | async-start | bytes 2097152 | tf_op jit(solution)/shard_map/all_to_all | solution.py:332
  9.9 1.5 %collective-permute-done = f32[8,16,128]{2,1,0:T(8,128)S(1)} collective-permute-done((f32[8,16,128]{2,1,0:T(8,128)}, f32[8,16,128]{2,1,0:T(8,128)S(1)}, u32[]{:S(2)}, u32[]{:S(2)}) %collective-permute-start) | collective-permute-done | bytes 65568 | tf_op jit(solution)/shard_map/ppermute | solution.py:323
  11.3 0.8 pad_maximum_fusion.refs_5_
  12.2 4.1 %collective-permute-start.3 = (f32[2,8,16,128]{3,2,1,0:T(8,128)S(1)}, f32[2,8,16,128]{3,2,1,0:T(8,128)S(1)}, u32[]{:S(2)}, u32[]{:S(2)}) collective-permute-start(f32[2,8,16,128]{3,2,1,0:T(8,128)S(1)} %pad_maximum_fusion.refs_5_), channel_id=1, source_target_pairs={{0,96},{16,112},{32,0},{48,16},{64,32},{80,48},{96,64},{112,80},{1... | collective-permute-start | bytes 393224 | tf_op jit(solution)/shard_map/ppermute | solution.py:328
  16.3 1.3 %collective-permute-start.1 = (f32[2,8,16,128]{3,2,1,0:T(8,128)S(1)}, f32[2,8,16,128]{3,2,1,0:T(8,128)S(1)}, u32[]{:S(2)}, u32[]{:S(2)}) collective-permute-start(f32[2,8,16,128]{3,2,1,0:T(8,128)S(1)} %pad_maximum_fusion.refs_5_), channel_id=1, source_target_pairs={{0,32},{16,48},{32,64},{48,80},{64,96},{80,112},{96,0},{112,16},{1... | collective-permute-start | bytes 393224 | tf_op jit(solution)/shard_map/ppermute | solution.py:328
  18.2 2.6 %pack_bonds.1.refs_3_ = bf16[128,128,128]{2,1,0:T(8,128)(2,1)S(1)} custom-call(s32[1]{0:T(128)S(6)} %copy.13.count_ref.refs_0_, s32[128,128,128]{2,1,0:T(8,128)} %bond_ref.1, s32[128,128,128]{2,1,0:T(8,128)} %broken_ref.1), custom_call_target="tpu_custom_call" | custom-call | tf_op jit(solution)/shard_map/pack_bonds/pallas_call | solution.py:111
  20.9 2.0 %copy-done = bf16[128,128,128]{2,1,0:T(8,128)(2,1)} copy-done((bf16[128,128,128]{2,1,0:T(8,128)(2,1)}, bf16[128,128,128]{2,1,0:T(8,128)(2,1)S(1)}, u32[]{:S(2)}) %copy-start) | copy-done | bytes 4194328
  22.8 1.3 %collective-permute-done.2.refs_7_ = f32[2,8,16,128]{3,2,1,0:T(8,128)S(1)} collective-permute-done((f32[2,8,16,128]{3,2,1,0:T(8,128)S(1)}, f32[2,8,16,128]{3,2,1,0:T(8,128)S(1)}, u32[]{:S(2)}, u32[]{:S(2)}) %collective-permute-start.2) | collective-permute-done | bytes 131104 | tf_op jit(solution)/shard_map/ppermute | solution.py:328
  24.2 1.4 %collective-permute-done.1.refs_6_ = f32[2,8,16,128]{3,2,1,0:T(8,128)S(1)} collective-permute-done((f32[2,8,16,128]{3,2,1,0:T(8,128)S(1)}, f32[2,8,16,128]{3,2,1,0:T(8,128)S(1)}, u32[]{:S(2)}, u32[]{:S(2)}) %collective-permute-start.1) | collective-permute-done | bytes 131104 | tf_op jit(solution)/shard_map/ppermute | solution.py:328
  25.6 1.8 %all-to-all-done.refs_4_ = f32[16,8,16,128]{3,2,1,0:T(8,128)S(1)} async-done(((f32[16,8,16,128]{3,2,1,0:T(8,128)}), f32[16,8,16,128]{3,2,1,0:T(8,128)S(1)}, u32[]{:S(2)}, u32[]{:S(2)}) %all-to-all-start) | async-done | bytes 1048608 | tf_op jit(solution)/shard_map/all_to_all | solution.py:332
  27.4 6.2 %pair_forces.2 = (f32[768,128]{1,0:T(8,128)}, f32[4,3,16,128]{3,2,1,0:T(8,128)S(1)}, f32[4,3,16,128]{3,2,1,0:T(8,128)S(1)}) custom-call(s32[1]{0:T(128)S(6)} %copy.13.count_ref.refs_0_, s32[128]{0:T(128)S(1)} %copy-done.3, s32[128]{0:T(128)S(1)} %copy-done.4, bf16[128,128,128]{2,1,0:T(8,128)(2,1)} %copy-done, f32[16,8,16,128]{3,2,1,0:T(8,128)S(1)} %all-to-all-done.refs_4_, ...), custom_call_target="tpu_custom_call" | custom-call | tf_op jit(solution)/shard_map/pair_forces/pallas_call | solution.py:202
  33.6 0.6 copy-done.2
  34.2 7.2 %all-to-all-start.1 = ((f32[16,3,16,128]{3,2,1,0:T(8,128)}), f32[16,3,16,128]{3,2,1,0:T(8,128)S(1)}, u32[]{:S(2)}, u32[]{:S(2)}) async-start(f32[16,3,16,128]{3,2,1,0:T(8,128)} %bitcast.3), calls=%async_computation.1 | async-start | bytes 786432 | tf_op jit(solution)/shard_map/all_to_all | solution.py:332
  41.4 0.1 collective-permute-start.4
  41.5 1.3 %collective-permute-done.4.other_ref = f32[4,3,16,128]{3,2,1,0:T(8,128)S(1)} collective-permute-done((f32[4,3,16,128]{3,2,1,0:T(8,128)S(1)}, f32[4,3,16,128]{3,2,1,0:T(8,128)S(1)}, u32[]{:S(2)}, u32[]{:S(2)}) %collective-permute-start.4) | collective-permute-done | bytes 98336 | tf_op jit(solution)/shard_map/ppermute | solution.py:323
  42.8 0.6 copy-done.7
  43.4 1.6 %column_shares.2 = (f32[3,16,128]{2,1,0:T(8,128)}, f32[3,16,128]{2,1,0:T(8,128)}, f32[3,16,128]{2,1,0:T(8,128)}, f32[3,16,128]{2,1,0:T(8,128)}) custom-call(f32[4,3,16,128]{3,2,1,0:T(8,128)} %copy-done.2, f32[4,3,16,128]{3,2,1,0:T(8,128)} %copy-done.7), custom_call_target="tpu_custom_call" | custom-call | tf_op jit(solution)/shard_map/column_shares/pallas_call | solution.py:258
  45.0 1.2 %collective-permute-start.5 = (f32[3,16,128]{2,1,0:T(8,128)}, f32[3,16,128]{2,1,0:T(8,128)S(1)}, u32[]{:S(2)}, u32[]{:S(2)}) collective-permute-start(f32[3,16,128]{2,1,0:T(8,128)} %get-tuple-element.30), channel_id=1, source_target_pairs={{0,32},{16,48},{32,64},{48,80},{64,96},{80,112},{96,0},{112,16},{1... | collective-permute-start | bytes 73736 | tf_op jit(solution)/shard_map/ppermute | solution.py:328
  46.3 4.0 %collective-permute-start.6 = (f32[3,16,128]{2,1,0:T(8,128)}, f32[3,16,128]{2,1,0:T(8,128)S(1)}, u32[]{:S(2)}, u32[]{:S(2)}) collective-permute-start(f32[3,16,128]{2,1,0:T(8,128)} %get-tuple-element.31), channel_id=1, source_target_pairs={{0,64},{16,80},{32,96},{48,112},{64,0},{80,16},{96,32},{112,48},{1... | collective-permute-start | bytes 73736 | tf_op jit(solution)/shard_map/ppermute | solution.py:328
  50.2 2.6 %collective-permute-start.7 = (f32[3,16,128]{2,1,0:T(8,128)}, f32[3,16,128]{2,1,0:T(8,128)S(1)}, u32[]{:S(2)}, u32[]{:S(2)}) collective-permute-start(f32[3,16,128]{2,1,0:T(8,128)} %get-tuple-element.32), channel_id=1, source_target_pairs={{0,96},{16,112},{32,0},{48,16},{64,32},{80,48},{96,64},{112,80},{1... | collective-permute-start | bytes 73736 | tf_op jit(solution)/shard_map/ppermute | solution.py:328
  52.9 1.7 %collective-permute-done.7.refs_3_ = f32[3,16,128]{2,1,0:T(8,128)S(1)} collective-permute-done((f32[3,16,128]{2,1,0:T(8,128)}, f32[3,16,128]{2,1,0:T(8,128)S(1)}, u32[]{:S(2)}, u32[]{:S(2)}) %collective-permute-start.7) | collective-permute-done | bytes 24608 | tf_op jit(solution)/shard_map/ppermute | solution.py:328
  54.6 0.6 copy-done.12
  55.2 0.2 copy-done.5
  55.4 1.9 %next_step.1 = (f32[16,3,16,128]{3,2,1,0:T(8,128)}, f32[3,16,128]{2,1,0:T(8,128)}, f32[3,16,128]{2,1,0:T(8,128)}, f32[3,16,128]{2,1,0:T(8,128)}) custom-call(f32[16,3,16,128]{3,2,1,0:T(8,128)} %copy-done.5, f32[3,16,128]{2,1,0:T(8,128)} %get-tuple-element.29.refs_0_, f32[3,16,128]{2,1,0:T(8,128)} %copy-done.9, f32[3,16,128]{2,1,0:T(8,128)} %copy-done.10, ...), custom_call_target="tpu_custom_call" | custom-call | tf_op jit(solution)/shard_map/next_step/pallas_call | solution.py:291
  57.3 6.9 %all-to-all-start.2 = ((f32[16,3,16,128]{3,2,1,0:T(8,128)}), f32[16,3,16,128]{3,2,1,0:T(8,128)S(1)}, u32[]{:S(2)}, u32[]{:S(2)}) async-start(f32[16,3,16,128]{3,2,1,0:T(8,128)} %get-tuple-element.35), calls=%async_computation.2 | async-start | bytes 786432 | tf_op jit(solution)/shard_map/all_to_all | solution.py:332
  64.3 1.4 %collective-permute-done.8 = f32[3,16,128]{2,1,0:T(8,128)S(1)} collective-permute-done((f32[3,16,128]{2,1,0:T(8,128)}, f32[3,16,128]{2,1,0:T(8,128)S(1)}, u32[]{:S(2)}, u32[]{:S(2)}) %collective-permute-start.8) | collective-permute-done | bytes 24608 | tf_op jit(solution)/shard_map/ppermute | solution.py:323
  65.6 0.7 pad_maximum_fusion.1.refs_10_
  66.4 3.5 %collective-permute-start.11 = (f32[2,3,16,128]{3,2,1,0:T(8,128)S(1)}, f32[2,3,16,128]{3,2,1,0:T(8,128)S(1)}, u32[]{:S(2)}, u32[]{:S(2)}) collective-permute-start(f32[2,3,16,128]{3,2,1,0:T(8,128)S(1)} %pad_maximum_fusion.1.refs_10_), channel_id=1, source_target_pairs={{0,96},{16,112},{32,0},{48,16},{64,32},{80,48},{96,64},{112,80},{1... | collective-permute-start | bytes 147464 | tf_op jit(solution)/shard_map/ppermute | solution.py:328
  69.9 0.9 collective-permute-start.9
  70.8 1.6 %collective-permute-done.11.refs_13_ = f32[2,3,16,128]{3,2,1,0:T(8,128)S(1)} collective-permute-done((f32[2,3,16,128]{3,2,1,0:T(8,128)S(1)}, f32[2,3,16,128]{3,2,1,0:T(8,128)S(1)}, u32[]{:S(2)}, u32[]{:S(2)}) %collective-permute-start.11) | collective-permute-done | bytes 49184 | tf_op jit(solution)/shard_map/ppermute | solution.py:328
  72.3 3.2 %collective-permute-done.10.refs_12_ = f32[2,3,16,128]{3,2,1,0:T(8,128)S(1)} collective-permute-done((f32[2,3,16,128]{3,2,1,0:T(8,128)S(1)}, f32[2,3,16,128]{3,2,1,0:T(8,128)S(1)}, u32[]{:S(2)}, u32[]{:S(2)}) %collective-permute-start.10) | collective-permute-done | bytes 49184 | tf_op jit(solution)/shard_map/ppermute | solution.py:328
  75.6 0.2 collective-permute-done.9.refs_11_
  75.7 6.2 %pair_forces.3 = (f32[768,128]{1,0:T(8,128)}, f32[4,3,16,128]{3,2,1,0:T(8,128)S(1)}, f32[4,3,16,128]{3,2,1,0:T(8,128)S(1)}) custom-call(s32[1]{0:T(128)S(6)} %copy.13.count_ref.refs_0_, s32[128]{0:T(128)S(1)} %copy-done.3, s32[128]{0:T(128)S(1)} %copy-done.4, bf16[128,128,128]{2,1,0:T(8,128)(2,1)} %copy-done, f32[16,8,16,128]{3,2,1,0:T(8,128)S(1)} %all-to-all-done.refs_4_, ...), custom_call_target="tpu_custom_call" | custom-call | tf_op jit(solution)/shard_map/pair_forces/pallas_call | solution.py:202
  81.9 0.6 copy-done.1
  82.5 9.0 %all-to-all-start.3 = ((f32[16,3,16,128]{3,2,1,0:T(8,128)}), f32[16,3,16,128]{3,2,1,0:T(8,128)S(1)}, u32[]{:S(2)}, u32[]{:S(2)}) async-start(f32[16,3,16,128]{3,2,1,0:T(8,128)} %bitcast.6), calls=%async_computation.3 | async-start | bytes 786432 | tf_op jit(solution)/shard_map/all_to_all | solution.py:332
  91.5 0.1 collective-permute-start.12
  91.6 1.3 %collective-permute-done.12.other_ref = f32[4,3,16,128]{3,2,1,0:T(8,128)S(1)} collective-permute-done((f32[4,3,16,128]{3,2,1,0:T(8,128)S(1)}, f32[4,3,16,128]{3,2,1,0:T(8,128)S(1)}, u32[]{:S(2)}, u32[]{:S(2)}) %collective-permute-start.12) | collective-permute-done | bytes 98336 | tf_op jit(solution)/shard_map/ppermute | solution.py:323
  92.9 0.6 copy-done.8
  93.6 1.6 %column_shares.3 = (f32[3,16,128]{2,1,0:T(8,128)}, f32[3,16,128]{2,1,0:T(8,128)}, f32[3,16,128]{2,1,0:T(8,128)}, f32[3,16,128]{2,1,0:T(8,128)}) custom-call(f32[4,3,16,128]{3,2,1,0:T(8,128)} %copy-done.1, f32[4,3,16,128]{3,2,1,0:T(8,128)} %copy-done.8), custom_call_target="tpu_custom_call" | custom-call | tf_op jit(solution)/shard_map/column_shares/pallas_call | solution.py:258
  95.1 1.8 %collective-permute-start.14 = (f32[3,16,128]{2,1,0:T(8,128)}, f32[3,16,128]{2,1,0:T(8,128)S(1)}, u32[]{:S(2)}, u32[]{:S(2)}) collective-permute-start(f32[3,16,128]{2,1,0:T(8,128)} %get-tuple-element.42), channel_id=1, source_target_pairs={{0,64},{16,80},{32,96},{48,112},{64,0},{80,16},{96,32},{112,48},{1... | collective-permute-start | bytes 73736 | tf_op jit(solution)/shard_map/ppermute | solution.py:328
  96.9 2.6 %collective-permute-start.15 = (f32[3,16,128]{2,1,0:T(8,128)}, f32[3,16,128]{2,1,0:T(8,128)S(1)}, u32[]{:S(2)}, u32[]{:S(2)}) collective-permute-start(f32[3,16,128]{2,1,0:T(8,128)} %get-tuple-element.43), channel_id=1, source_target_pairs={{0,96},{16,112},{32,0},{48,16},{64,32},{80,48},{96,64},{112,80},{1... | collective-permute-start | bytes 73736 | tf_op jit(solution)/shard_map/ppermute | solution.py:328
  99.6 0.8 collective-permute-done.13.refs_1_
  100.4 0.3 collective-permute-done.14.refs_2_
  100.7 0.8 collective-permute-done.15.refs_3_
  101.5 0.6 copy-done.14
  102.1 0.1 copy-done.6
  102.3 1.7 %last_half_step.1 = (f32[3,2048]{1,0:T(4,128)}, f32[3,2048]{1,0:T(4,128)}) custom-call(f32[16,3,16,128]{3,2,1,0:T(8,128)} %copy-done.6, f32[3,16,128]{2,1,0:T(8,128)} %get-tuple-element.40.refs_0_, f32[3,16,128]{2,1,0:T(8,128)} %copy-done.11, f32[3,16,128]{2,1,0:T(8,128)} %copy-done.13, f32[3,16,128]{2,1,0:T(8,128)} %copy-done.14, ...), custom_call_target="tpu_custom_call" | custom-call | tf_op jit(solution)/shard_map/last_half_step/pallas_call | solution.py:313
  (32 shorter events, 0.2 us)
Async XLA Ops:
  2.7 24.8 %all-to-all-start = ((f32[16,8,16,128]{3,2,1,0:T(8,128)}), f32[16,8,16,128]{3,2,1,0:T(8,128)S(1)}, u32[]{:S(2)}, u32[]{:S(2)}) async-start(f32[16,8,16,128]{3,2,1,0:T(8,128)} %get-tuple-element.24), calls=%async_computation | async-start | bytes 2097152 | tf_op jit(solution)/shard_map/all_to_all | solution.py:332
  9.8 1.5 %collective-permute-start = (f32[8,16,128]{2,1,0:T(8,128)}, f32[8,16,128]{2,1,0:T(8,128)S(1)}, u32[]{:S(2)}, u32[]{:S(2)}) collective-permute-start(f32[8,16,128]{2,1,0:T(8,128)} %get-tuple-element.25.refs_4_), channel_id=1, source_target_pairs={{0,16},{16,0},{32,48},{48,32},{64,80},{80,64},{96,112},{112,96},{1... | collective-permute-start | bytes 196616 | tf_op jit(solution)/shard_map/ppermute | solution.py:323
  12.2 10.6 %collective-permute-start.3 = (f32[2,8,16,128]{3,2,1,0:T(8,128)S(1)}, f32[2,8,16,128]{3,2,1,0:T(8,128)S(1)}, u32[]{:S(2)}, u32[]{:S(2)}) collective-permute-start(f32[2,8,16,128]{3,2,1,0:T(8,128)S(1)} %pad_maximum_fusion.refs_5_), channel_id=1, source_target_pairs={{0,96},{16,112},{32,0},{48,16},{64,32},{80,48},{96,64},{112,80},{1... | collective-permute-start | bytes 393224 | tf_op jit(solution)/shard_map/ppermute | solution.py:328
  16.3 7.9 %collective-permute-start.2 = (f32[2,8,16,128]{3,2,1,0:T(8,128)S(1)}, f32[2,8,16,128]{3,2,1,0:T(8,128)S(1)}, u32[]{:S(2)}, u32[]{:S(2)}) collective-permute-start(f32[2,8,16,128]{3,2,1,0:T(8,128)S(1)} %pad_maximum_fusion.refs_5_), channel_id=1, source_target_pairs={{0,64},{16,80},{32,96},{48,112},{64,0},{80,16},{96,32},{112,48},{1... | collective-permute-start | bytes 393224 | tf_op jit(solution)/shard_map/ppermute | solution.py:328
  16.3 9.3 %collective-permute-start.1 = (f32[2,8,16,128]{3,2,1,0:T(8,128)S(1)}, f32[2,8,16,128]{3,2,1,0:T(8,128)S(1)}, u32[]{:S(2)}, u32[]{:S(2)}) collective-permute-start(f32[2,8,16,128]{3,2,1,0:T(8,128)S(1)} %pad_maximum_fusion.refs_5_), channel_id=1, source_target_pairs={{0,32},{16,48},{32,64},{48,80},{64,96},{80,112},{96,0},{112,16},{1... | collective-permute-start | bytes 393224 | tf_op jit(solution)/shard_map/ppermute | solution.py:328
  18.2 9.2 %copy-start.3 = (s32[128]{0:T(128)S(1)}, s32[128]{0:T(128)}, u32[]{:S(2)}) copy-start(s32[128]{0:T(128)} %refs_1_.3) | copy-start | bytes 1540
  18.2 9.2 %copy-start.4 = (s32[128]{0:T(128)S(1)}, s32[128]{0:T(128)}, u32[]{:S(2)}) copy-start(s32[128]{0:T(128)} %refs_2_.3) | copy-start | bytes 1540
  20.9 2.0 %copy-start = (bf16[128,128,128]{2,1,0:T(8,128)(2,1)}, bf16[128,128,128]{2,1,0:T(8,128)(2,1)S(1)}, u32[]{:S(2)}) copy-start(bf16[128,128,128]{2,1,0:T(8,128)(2,1)S(1)} %pack_bonds.1.refs_3_) | copy-start | bytes 12582916
  33.6 0.6 copy-start.2
  34.2 20.4 %all-to-all-start.1 = ((f32[16,3,16,128]{3,2,1,0:T(8,128)}), f32[16,3,16,128]{3,2,1,0:T(8,128)S(1)}, u32[]{:S(2)}, u32[]{:S(2)}) async-start(f32[16,3,16,128]{3,2,1,0:T(8,128)} %bitcast.3), calls=%async_computation.1 | async-start | bytes 786432 | tf_op jit(solution)/shard_map/all_to_all | solution.py:332
  41.4 1.4 %collective-permute-start.4 = (f32[4,3,16,128]{3,2,1,0:T(8,128)S(1)}, f32[4,3,16,128]{3,2,1,0:T(8,128)S(1)}, u32[]{:S(2)}, u32[]{:S(2)}) collective-permute-start(f32[4,3,16,128]{3,2,1,0:T(8,128)S(1)} %get-tuple-element.28), channel_id=1, source_target_pairs={{0,16},{16,0},{32,48},{48,32},{64,80},{80,64},{96,112},{112,96},{1... | collective-permute-start | bytes 294920 | tf_op jit(solution)/shard_map/ppermute | solution.py:323
  42.8 0.6 copy-start.7
  45.0 7.8 %collective-permute-start.5 = (f32[3,16,128]{2,1,0:T(8,128)}, f32[3,16,128]{2,1,0:T(8,128)S(1)}, u32[]{:S(2)}, u32[]{:S(2)}) collective-permute-start(f32[3,16,128]{2,1,0:T(8,128)} %get-tuple-element.30), channel_id=1, source_target_pairs={{0,32},{16,48},{32,64},{48,80},{64,96},{80,112},{96,0},{112,16},{1... | collective-permute-start | bytes 73736 | tf_op jit(solution)/shard_map/ppermute | solution.py:328
  46.3 6.6 %collective-permute-start.6 = (f32[3,16,128]{2,1,0:T(8,128)}, f32[3,16,128]{2,1,0:T(8,128)S(1)}, u32[]{:S(2)}, u32[]{:S(2)}) collective-permute-start(f32[3,16,128]{2,1,0:T(8,128)} %get-tuple-element.31), channel_id=1, source_target_pairs={{0,64},{16,80},{32,96},{48,112},{64,0},{80,16},{96,32},{112,48},{1... | collective-permute-start | bytes 73736 | tf_op jit(solution)/shard_map/ppermute | solution.py:328
  50.2 4.4 %collective-permute-start.7 = (f32[3,16,128]{2,1,0:T(8,128)}, f32[3,16,128]{2,1,0:T(8,128)S(1)}, u32[]{:S(2)}, u32[]{:S(2)}) collective-permute-start(f32[3,16,128]{2,1,0:T(8,128)} %get-tuple-element.32), channel_id=1, source_target_pairs={{0,96},{16,112},{32,0},{48,16},{64,32},{80,48},{96,64},{112,80},{1... | collective-permute-start | bytes 73736 | tf_op jit(solution)/shard_map/ppermute | solution.py:328
  52.9 1.7 %copy-start.9 = (f32[3,16,128]{2,1,0:T(8,128)}, f32[3,16,128]{2,1,0:T(8,128)S(1)}, u32[]{:S(2)}) copy-start(f32[3,16,128]{2,1,0:T(8,128)S(1)} %collective-permute-done.5.refs_1_) | copy-start | bytes 73732
  52.9 1.7 %copy-start.10 = (f32[3,16,128]{2,1,0:T(8,128)}, f32[3,16,128]{2,1,0:T(8,128)S(1)}, u32[]{:S(2)}) copy-start(f32[3,16,128]{2,1,0:T(8,128)S(1)} %collective-permute-done.6.refs_2_) | copy-start | bytes 73732
  54.6 0.6 copy-start.12
  54.6 0.8 copy-start.5
  57.3 18.4 %all-to-all-start.2 = ((f32[16,3,16,128]{3,2,1,0:T(8,128)}), f32[16,3,16,128]{3,2,1,0:T(8,128)S(1)}, u32[]{:S(2)}, u32[]{:S(2)}) async-start(f32[16,3,16,128]{3,2,1,0:T(8,128)} %get-tuple-element.35), calls=%async_computation.2 | async-start | bytes 786432 | tf_op jit(solution)/shard_map/all_to_all | solution.py:332
  64.2 1.5 %collective-permute-start.8 = (f32[3,16,128]{2,1,0:T(8,128)}, f32[3,16,128]{2,1,0:T(8,128)S(1)}, u32[]{:S(2)}, u32[]{:S(2)}) collective-permute-start(f32[3,16,128]{2,1,0:T(8,128)} %get-tuple-element.36), channel_id=1, source_target_pairs={{0,16},{16,0},{32,48},{48,32},{64,80},{80,64},{96,112},{112,96},{1... | collective-permute-start | bytes 73736 | tf_op jit(solution)/shard_map/ppermute | solution.py:323
  66.4 5.9 %collective-permute-start.11 = (f32[2,3,16,128]{3,2,1,0:T(8,128)S(1)}, f32[2,3,16,128]{3,2,1,0:T(8,128)S(1)}, u32[]{:S(2)}, u32[]{:S(2)}) collective-permute-start(f32[2,3,16,128]{3,2,1,0:T(8,128)S(1)} %pad_maximum_fusion.1.refs_10_), channel_id=1, source_target_pairs={{0,96},{16,112},{32,0},{48,16},{64,32},{80,48},{96,64},{112,80},{1... | collective-permute-start | bytes 147464 | tf_op jit(solution)/shard_map/ppermute | solution.py:328
  69.9 5.6 %collective-permute-start.10 = (f32[2,3,16,128]{3,2,1,0:T(8,128)S(1)}, f32[2,3,16,128]{3,2,1,0:T(8,128)S(1)}, u32[]{:S(2)}, u32[]{:S(2)}) collective-permute-start(f32[2,3,16,128]{3,2,1,0:T(8,128)S(1)} %pad_maximum_fusion.1.refs_10_), channel_id=1, source_target_pairs={{0,64},{16,80},{32,96},{48,112},{64,0},{80,16},{96,32},{112,48},{1... | collective-permute-start | bytes 147464 | tf_op jit(solution)/shard_map/ppermute | solution.py:328
  69.9 5.8 %collective-permute-start.9 = (f32[2,3,16,128]{3,2,1,0:T(8,128)S(1)}, f32[2,3,16,128]{3,2,1,0:T(8,128)S(1)}, u32[]{:S(2)}, u32[]{:S(2)}) collective-permute-start(f32[2,3,16,128]{3,2,1,0:T(8,128)S(1)} %pad_maximum_fusion.1.refs_10_), channel_id=1, source_target_pairs={{0,32},{16,48},{32,64},{48,80},{64,96},{80,112},{96,0},{112,16},{1... | collective-permute-start | bytes 147464 | tf_op jit(solution)/shard_map/ppermute | solution.py:328
  81.9 0.6 copy-start.1
  82.5 19.0 %all-to-all-start.3 = ((f32[16,3,16,128]{3,2,1,0:T(8,128)}), f32[16,3,16,128]{3,2,1,0:T(8,128)S(1)}, u32[]{:S(2)}, u32[]{:S(2)}) async-start(f32[16,3,16,128]{3,2,1,0:T(8,128)} %bitcast.6), calls=%async_computation.3 | async-start | bytes 786432 | tf_op jit(solution)/shard_map/all_to_all | solution.py:332
  91.5 1.4 %collective-permute-start.12 = (f32[4,3,16,128]{3,2,1,0:T(8,128)S(1)}, f32[4,3,16,128]{3,2,1,0:T(8,128)S(1)}, u32[]{:S(2)}, u32[]{:S(2)}) collective-permute-start(f32[4,3,16,128]{3,2,1,0:T(8,128)S(1)} %get-tuple-element.39), channel_id=1, source_target_pairs={{0,16},{16,0},{32,48},{48,32},{64,80},{80,64},{96,112},{112,96},{1... | collective-permute-start | bytes 294920 | tf_op jit(solution)/shard_map/ppermute | solution.py:323
  92.9 0.6 copy-start.8
  95.1 5.2 %collective-permute-start.13 = (f32[3,16,128]{2,1,0:T(8,128)}, f32[3,16,128]{2,1,0:T(8,128)S(1)}, u32[]{:S(2)}, u32[]{:S(2)}) collective-permute-start(f32[3,16,128]{2,1,0:T(8,128)} %get-tuple-element.41), channel_id=1, source_target_pairs={{0,32},{16,48},{32,64},{48,80},{64,96},{80,112},{96,0},{112,16},{1... | collective-permute-start | bytes 73736 | tf_op jit(solution)/shard_map/ppermute | solution.py:328
  95.1 5.5 %collective-permute-start.14 = (f32[3,16,128]{2,1,0:T(8,128)}, f32[3,16,128]{2,1,0:T(8,128)S(1)}, u32[]{:S(2)}, u32[]{:S(2)}) collective-permute-start(f32[3,16,128]{2,1,0:T(8,128)} %get-tuple-element.42), channel_id=1, source_target_pairs={{0,64},{16,80},{32,96},{48,112},{64,0},{80,16},{96,32},{112,48},{1... | collective-permute-start | bytes 73736 | tf_op jit(solution)/shard_map/ppermute | solution.py:328
  96.9 4.6 %collective-permute-start.15 = (f32[3,16,128]{2,1,0:T(8,128)}, f32[3,16,128]{2,1,0:T(8,128)S(1)}, u32[]{:S(2)}, u32[]{:S(2)}) collective-permute-start(f32[3,16,128]{2,1,0:T(8,128)} %get-tuple-element.43), channel_id=1, source_target_pairs={{0,96},{16,112},{32,0},{48,16},{64,32},{80,48},{96,64},{112,80},{1... | collective-permute-start | bytes 73736 | tf_op jit(solution)/shard_map/ppermute | solution.py:328
  100.4 1.1 %copy-start.11 = (f32[3,16,128]{2,1,0:T(8,128)}, f32[3,16,128]{2,1,0:T(8,128)S(1)}, u32[]{:S(2)}) copy-start(f32[3,16,128]{2,1,0:T(8,128)S(1)} %collective-permute-done.13.refs_1_) | copy-start | bytes 73732
  100.7 0.8 copy-start.13
  101.5 0.6 copy-start.14
  101.5 0.7 copy-start.6
